TPU v7x, 32 devices: a whole 2x2x4 slice. The times are simulated.
32 devices in a mesh: batch: 8 (over y, x, core), mp: 4 (over z).
Axes of the slice: x: 2, y: 2, z: 4, core: 2. Of those that a mesh axis runs over, the one named last changes fastest.
Arguments:
- residual: bfloat16 [8, 64, 8192], P('batch', None, 'mp'), may hold values from -6 to 6
- query_states: bfloat16 [8, 64, 4096], P('batch', None, 'mp')
- key_states: bfloat16 [8, 64, 512], P('batch')
- value_states: bfloat16 [8, 64, 512], P('batch'), may hold values from -6 to 6
- prompt_perm: int32 [8], replicated, may hold values from 0 to 7, each once
- ablated_heads: int32 [8], replicated, may hold values from 0 to 31, as said below
- out_weight: bfloat16 [4096, 8192], P('batch', 'mp'), may hold values from -0.09375 to 0.09375
- rms_gain: float32 [8192], P('mp'), may hold values from 0.1 to 1.9
- gate_weight: bfloat16 [8192, 14336], P('mp', 'batch'), may hold values from -0.0625 to 0.0625
- up_weight: bfloat16 [8192, 14336], P('mp', 'batch'), may hold values from -0.0625 to 0.0625
- down_weight: bfloat16 [14336, 8192], P('batch', 'mp'), may hold values from -0.046875 to 0.046875
Outputs:
- attn_out: bfloat16 [8, 64, 8192], P('batch', None, 'mp')
- mlp_out: bfloat16 [8, 64, 8192], P('batch', None, 'mp')
Inputs may be any that keep to these rules, and one draw needn't show every extreme that they name: `prompt_perm`: each prompt index appears exactly once. `ablated_heads`: 8 different head indices in any order, one of them 32 - 1.
All inputs are finite; a program needn't handle non-finite values.
Results may differ from a plain program's by a relative error of at most 0.035.
Values may be sent and summed in bfloat16 or wider, within the bound.
A program may use at most 128 MiB of HBM per device.

v0:
```python
import math
import jax
import jax.numpy as jnp
from jax import lax
from jax.sharding import PartitionSpec as P

D = 8192
HEADS = 32
KV = 4
HD = 128
ABLATED = 8


def local_heads(query_states, key_states, value_states):
    prompts_here, length, columns = query_states.shape
    head_count = columns // HD
    first_head = lax.axis_index("mp") * head_count
    owners = (first_head + jnp.arange(head_count)) // (HEADS // KV)
    query_four = query_states.reshape(prompts_here, length, head_count, HD)
    key_four = jnp.take(key_states.reshape(prompts_here, length, KV, HD), owners, axis=2)
    value_four = jnp.take(value_states.reshape(prompts_here, length, KV, HD), owners, axis=2)
    scores = jnp.einsum(
        "pshd,pthd->phst", query_four, key_four, preferred_element_type=jnp.float32
    ) / math.sqrt(HD)
    positions = jnp.arange(length)
    causal = positions[:, None] >= positions[None, :]
    scores = jnp.where(causal, scores, -1e30)
    highest = jnp.max(scores, axis=-1, keepdims=True)
    weights = jnp.exp(scores - highest)
    probability = (weights / jnp.sum(weights, axis=-1, keepdims=True)).astype(jnp.bfloat16)
    mixed_heads = jnp.einsum(
        "phst,pthd->pshd", probability, value_four, preferred_element_type=jnp.float32
    )
    return mixed_heads.astype(jnp.bfloat16).reshape(prompts_here, length, head_count * HD)


def body(
    residual,
    query_states,
    key_states,
    value_states,
    prompt_perm,
    ablated_heads,
    out_weight,
    rms_gain,
    gate_weight,
    up_weight,
    down_weight,
):
    prompts_here, length, model_cols = residual.shape
    local_rows = prompts_here * length
    head_block = local_heads(query_states, key_states, value_states)
    all_heads = lax.all_gather(head_block, "mp", axis=2, tiled=True)
    batch_index = lax.axis_index("batch")
    sources = jnp.take(prompt_perm, batch_index * prompts_here + jnp.arange(prompts_here))
    stacked = all_heads.reshape(prompts_here, length, HEADS, HD)
    picked_cols = jnp.take(stacked, ablated_heads, axis=2).reshape(
        prompts_here, length * ABLATED * HD
    )
    block_rows = lax.all_gather(picked_cols, "batch", axis=0, tiled=True)
    selector = (sources[:, None] == jnp.arange(block_rows.shape[0])[None, :]).astype(jnp.bfloat16)
    picked = jnp.dot(selector, block_rows, preferred_element_type=jnp.float32)
    picked_four = picked.astype(jnp.bfloat16).reshape(prompts_here, length, ABLATED, HD)
    placing = (jnp.arange(HEADS)[:, None] == ablated_heads[None, :]).astype(jnp.bfloat16)
    placed = jnp.einsum(
        "psad,ga->psgd", picked_four, placing, preferred_element_type=jnp.float32
    ).astype(jnp.bfloat16)
    chosen = jnp.any(jnp.arange(HEADS)[:, None] == ablated_heads[None, :], axis=1)
    mixed_heads = jnp.where(chosen[None, None, :, None], placed, stacked).reshape(
        local_rows, HEADS * HD
    )
    attn_float = jnp.dot(
        mixed_heads,
        lax.all_gather(out_weight, "batch", axis=0, tiled=True),
        preferred_element_type=jnp.float32,
    )
    attn_out = attn_float.astype(jnp.bfloat16)
    hidden_state = residual.reshape(local_rows, model_cols).astype(jnp.float32) + attn_float
    squares = lax.psum(jnp.sum(hidden_state * hidden_state, axis=1), "mp")
    inverse = lax.rsqrt(squares / D + 1e-05)
    normed = (hidden_state * inverse[:, None] * rms_gain[None, :]).astype(jnp.bfloat16)
    block_rows = lax.all_gather(normed, "batch", axis=0, tiled=True)
    gate_part = jnp.dot(block_rows, gate_weight, preferred_element_type=jnp.float32)
    up_part = jnp.dot(block_rows, up_weight, preferred_element_type=jnp.float32)
    partial_value = jnp.concatenate([gate_part, up_part], axis=1)
    slice_width = gate_weight.shape[1]
    summed = lax.psum(partial_value.astype(jnp.bfloat16), "mp").astype(jnp.float32)
    hidden = (jax.nn.silu(summed[:, :slice_width]) * summed[:, slice_width:]).astype(jnp.bfloat16)
    block_rows = hidden
    mlp_float = lax.psum_scatter(
        jnp.dot(block_rows, down_weight, preferred_element_type=jnp.float32).astype(jnp.bfloat16),
        "batch",
        scatter_dimension=0,
        tiled=True,
    )
    return (
        attn_out.reshape(prompts_here, length, model_cols),
        mlp_float.reshape(prompts_here, length, model_cols),
    )


def solution(mesh):
    placed = (
        P("batch", None, "mp"),
        P("batch", None, "mp"),
        P("batch", None, None),
        P("batch", None, None),
        P(),
        P(),
        P("batch", "mp"),
        P("mp"),
        P("mp", "batch"),
        P("mp", "batch"),
        P("batch", "mp"),
    )
    return jax.shard_map(
        body,
        mesh=mesh,
        in_specs=placed,
        out_specs=(P("batch", None, "mp"), P("batch", None, "mp")),
        check_vma=False,
    )
```

profile of v0, /device:TPU:0, one launch (start us, length us, event | category | flops | bytes accessed | tf_op | source)
XLA Modules:
  0.0 413.6 jit_solution(484651136919230348)
XLA Ops:
  7.2 0.0 copy-start
  7.2 0.0 all-gather.9.cloned.1.call-start
  7.3 0.7 compare_select_fusion.1
  7.9 0.7 compare_and_fusion.1
  8.6 0.9 copy.37
  9.6 0.6 gather_fusion.2
  10.2 0.3 fusion.7
  10.4 0.1 fusion.41
  10.5 0.9 bitcast_bitcast_fusion.1
  11.4 0.6 gather_fusion.1
  11.9 0.0 copy-start.6
  12.0 0.0 copy-start.4
  12.0 0.3 fusion.9
  12.3 17.4 %all_gather.12 = bf16[1,64,4096]{2,1,0:T(8,128)(2,1)S(1)} all-gather(bf16[1,64,1024]{2,1,0:T(8,128)(2,1)S(1)} %bitcast.109), channel_id=1, replica_groups=mesh['batch'=8,'mp'=4] {'mp'}, dimensions={2}, use_global_device_ids=true | all-gather | bytes 655360 | tf_op jit(solution)/shard_map/all_gather | solution.py:53
  29.6 0.1 copy.38
  29.7 0.0 copy-start.2
  29.7 0.2 copy.30
  30.0 0.6 gather_fusion
  30.5 0.1 select_bitcast_fusion
  30.6 0.1 copy.31
  30.7 0.8 reshape.200
  31.5 0.0 all-gather.9.cloned.1.call-update
  31.5 0.0 all-gather.5.cloned.1.call-start
  31.6 0.7 all-gather.5.cloned.1.call-update
  32.3 0.0 all-gather.7.cloned.1.call-start
  32.3 0.6 dynamic-slice.2
  33.5 0.1 fusion.30
  33.6 27.7 %all-gather.9.cloned.1.call-done = bf16[8,1,65536]{2,1,0:T(2,128)(2,1)} async-done(((bf16[1,1,65536]{2,1,0:T(2,128)(2,1)}), bf16[8,1,65536]{2,1,0:T(2,128)(2,1)}) %all-gather.9.cloned.1.call-update) | async-done | bytes 1048592 | tf_op jit(solution)/shard_map/all_gather | solution.py:60
  61.3 2.9 fusion.11
  64.2 0.4 fusion.10
  64.6 88.5 %all-gather.5.cloned.1.call-done = bf16[4096,2048]{1,0:T(8,128)(2,1)} async-done(((bf16[512,2048]{1,0:T(8,128)(2,1)}), bf16[4096,2048]{1,0:T(8,128)(2,1)}) %all-gather.5.cloned.1.call-update) | async-done | bytes 16777232 | tf_op jit(solution)/shard_map/all_gather | solution.py:74
  153.1 8.9 %multiply_reduce_fusion = (f32[64]{0:T(128)S(1)}, f32[64,2048]{1,0:T(8,128)S(1)}) fusion(bf16[1,64,2048]{2,1,0:T(8,128)(2,1)S(1)} %copy-done.2, bf16[4096,2048]{1,0:T(8,128)(2,1)} %all-gather.5.cloned.1.call-done, bf16[8,8,32,128]{3,2,1,0:T(8,128)(2,1)S(1)} %bitcast.106), kind=kOutput, calls=%fused_computation.29 | convolution fusion | flops 1074266112 | bytes 18088192 | tf_op jit(solution)/shard_map/dot_general | solution.py:72
  162.0 11.7 %psum.14 = f32[64]{0:T(128)S(1)} all-reduce(f32[64]{0:T(128)S(1)} %get-tuple-element.16), channel_id=1, replica_groups=mesh['batch'=8,'mp'=4] {'mp'}, use_global_device_ids=true, to_apply=%region_4.6 | all-reduce | flops 64 | bytes 512 | tf_op jit(solution)/shard_map/psum | solution.py:79
  173.7 0.8 multiply_convert_fusion
  174.6 0.0 all-gather.7.cloned.1.call-update
  174.6 0.2 all-reduce.2.cloned.1.call-start
  174.8 25.1 %all-gather.7.cloned.1.call-done = bf16[512,2048]{1,0:T(8,128)(2,1)} async-done(((bf16[64,2048]{1,0:T(8,128)(2,1)}), bf16[512,2048]{1,0:T(8,128)(2,1)}) %all-gather.7.cloned.1.call-update) | async-done | bytes 2097168 | tf_op jit(solution)/shard_map/all_gather | solution.py:82
  199.9 7.8 %convolution_convert_fusion.1 = bf16[512,1792]{1,0:T(8,128)(2,1)S(1)} fusion(bf16[512,2048]{1,0:T(8,128)(2,1)} %all-gather.7.cloned.1.call-done, bf16[2048,1792]{1,0:T(8,128)(2,1)} %param.22), kind=kOutput, calls=%fused_computation.8 | convolution fusion | flops 3759013888 | bytes 11272192 | tf_op jit(solution)/shard_map/dot_general | solution.py:84
  207.7 7.0 %convolution_convert_fusion.2 = bf16[512,1792]{1,0:T(8,128)(2,1)S(1)} fusion(bf16[512,2048]{1,0:T(8,128)(2,1)S(1)} %copy-done.5, bf16[2048,1792]{1,0:T(8,128)(2,1)} %param.21), kind=kOutput, calls=%fused_computation.9 | convolution fusion | flops 3759013888 | bytes 11272192 | tf_op jit(solution)/shard_map/dot_general | solution.py:83
  214.7 2.1 pad_maximum_fusion
  216.8 0.0 all-reduce.2.cloned.1.call-update
  216.9 0.0 reduce-scatter.2.cloned.1.call-start
  216.9 138.2 %all-reduce.2.cloned.1.call-done = bf16[512,3584]{1,0:T(8,128)(2,1)} async-done(((bf16[512,3584]{1,0:T(8,128)(2,1)}), bf16[512,3584]{1,0:T(8,128)(2,1)}) %all-reduce.2.cloned.1.call-update) | async-done | bytes 3670032 | tf_op jit(solution)/shard_map/psum | solution.py:87
  355.1 3.0 convert_element_type.62
  358.1 0.0 copy-start.1
  358.1 8.5 %convolution_convert_fusion = bf16[512,2048]{1,0:T(8,128)(2,1)} fusion(bf16[1792,2048]{1,0:T(8,128)(2,1)} %param.23, f32[512,3584]{1,0:T(8,128)S(1)} %convert_element_type.62), kind=kOutput, calls=%fused_computation.7 | convolution fusion | flops 3764649984 | bytes 16777216 | tf_op jit(solution)/shard_map/dot_general | solution.py:91
  366.6 0.0 reduce-scatter.2.cloned.1.call-update
  366.7 40.4 %reduce-scatter.2.cloned.1.call-done = bf16[64,2048]{1,0:T(8,128)(2,1)} async-done(((bf16[512,2048]{1,0:T(8,128)(2,1)}), bf16[64,2048]{1,0:T(8,128)(2,1)}) %reduce-scatter.2.cloned.1.call-update) | async-done | bytes 262160 | tf_op jit(solution)/shard_map/reduce_scatter | solution.py:90
  (17 shorter events, 0.1 us)
Async XLA Ops:
  7.2 1.5 copy-start
  7.2 54.1 %all-gather.9.cloned.1.call-start = ((), (), s32[]{:S(2)}) async-start(), calls=%async_computation.5 | async-start | bytes 2359296 | tf_op jit(solution)/shard_map/all_gather | solution.py:60
  11.9 20.4 %copy-start.6 = (s32[8]{0:T(128)S(1)}, s32[8]{0:T(128)}, u32[]{:S(2)}) copy-start(s32[8]{0:T(128)} %param.17) | copy-start | bytes 100
  12.0 21.6 %copy-start.4 = (s32[8]{0:T(128)S(1)}, s32[8]{0:T(128)}, u32[]{:S(2)}) copy-start(s32[8]{0:T(128)} %param.18) | copy-start | bytes 100
  29.7 123.4 %copy-start.2 = (bf16[1,64,2048]{2,1,0:T(8,128)(2,1)S(1)}, bf16[1,64,2048]{2,1,0:T(8,128)(2,1)}, u32[]{:S(2)}) copy-start(bf16[1,64,2048]{2,1,0:T(8,128)(2,1)} %param.13) | copy-start | bytes 786436
  31.5 121.6 %all-gather.5.cloned.1.call-start = ((), (), s32[]{:S(2)}) async-start(), calls=%async_computation.1 | async-start | bytes 18874368 | tf_op jit(solution)/shard_map/all_gather | solution.py:74
  32.3 167.6 %all-gather.7.cloned.1.call-start = ((), (), s32[]{:S(2)}) async-start(), calls=%async_computation.2 | async-start | bytes 2359296 | tf_op jit(solution)/shard_map/all_gather | solution.py:82
  153.1 20.6 %copy-start.3 = (f32[2048]{0:T(1024)S(1)}, f32[2048]{0:T(1024)}, u32[]{:S(2)}) copy-start(f32[2048]{0:T(1024)} %param.20) | copy-start | bytes 24580
  174.6 180.5 %all-reduce.2.cloned.1.call-start = ((), (), s32[]{:S(2)}) async-start(), calls=%async_computation.3 | async-start | bytes 7340032 | tf_op jit(solution)/shard_map/psum | solution.py:87
  199.9 7.8 %copy-start.5 = (bf16[512,2048]{1,0:T(8,128)(2,1)S(1)}, bf16[512,2048]{1,0:T(8,128)(2,1)}, u32[]{:S(2)}) copy-start(bf16[512,2048]{1,0:T(8,128)(2,1)} %all-gather.7.cloned.1.call-done) | copy-start | bytes 6291460
  216.9 190.2 %reduce-scatter.2.cloned.1.call-start = ((), (), s32[]{:S(2)}) async-start(), calls=%async_computation.4 | async-start | bytes 2359296 | tf_op jit(solution)/shard_map/reduce_scatter | solution.py:90
  358.1 49.0 %copy-start.1 = (bf16[1,64,512]{2,1,0:T(8,128)(2,1)S(1)}, bf16[1,64,512]{2,1,0:T(8,128)(2,1)}, u32[]{:S(2)}) copy-start(bf16[1,64,512]{2,1,0:T(8,128)(2,1)} %param.15) | copy-start | bytes 196612
Sparse Core Ops, SparseCore 0:
  31.6 29.6 all-gather.8
  63.2 89.8 all-gather.4
  174.7 25.1 all-gather.6
  217.0 138.0 all-reduce.1
  366.8 40.2 reduce-scatter.1
where the time goes:
time: 414 us
  waiting for transfers between devices  321 us (78%)
  matrix products  36.1 us (9%)
  blocking collectives  29.1 us (7%)
  between operations  14.6 us (4%)
  other arithmetic  7.56 us (2%)
  local copies, waits for them, and re-layouts  5.31 us (1%)
    psum x1, waiting for transfers between devices, body(): lax.psum(partial_value.astype(jnp.bfloat16), 'mp').astype(jnp.float32)  138 us
    all_gather x1, waiting for transfers between devices, body(): lax.all_gather(out_weight, 'batch', axis=0, tiled=True)  88.5 us
    reduce_scatter x1, waiting for transfers between devices, body(): lax.psum_scatter(jnp.dot(block_rows, down_weight, preferred_element_type=...  40.4 us
    all_gather x1, waiting for transfers between devices, body(): block_rows = lax.all_gather(picked_cols, 'batch', axis=0, tiled=True)  27.7 us
    all_gather x1, waiting for transfers between devices, body(): block_rows = lax.all_gather(normed, 'batch', axis=0, tiled=True)  25.1 us
    all_gather x1, blocking collectives, body(): all_heads = lax.all_gather(head_block, 'mp', axis=2, tiled=True)  17.4 us
    psum x1, blocking collectives, body(): squares = lax.psum(jnp.sum(hidden_state * hidden_state, axis=1), 'mp')  11.7 us
    dot_general x1, matrix products, body(): jnp.dot(mixed_heads, lax.all_gather(out_weight, 'batch', axis=0, tiled=Tr...  8.92 us
  transfers between devices with their start and end apart: 5, of which 5 were waited for; matrix products, arithmetic and copies ran while one was open for 1% of the time, Pallas kernels for 0%

commit v1 on v0

--- a/solution.py
+++ b/solution.py
@@ -57,7 +57,14 @@
     picked_cols = jnp.take(stacked, ablated_heads, axis=2).reshape(
         prompts_here, length * ABLATED * HD
     )
-    block_rows = lax.all_gather(picked_cols, "batch", axis=0, tiled=True)
+    ring = [picked_cols]
+    for hop in range(7):
+        ring.append(lax.ppermute(ring[-1], "batch", [(dev, (dev + 1) % 8) for dev in range(8)]))
+    block_rows = jnp.roll(
+        jnp.concatenate(ring[::-1], axis=0),
+        (lax.axis_index("batch") + 1) * ring[0].shape[0],
+        axis=0,
+    )
     selector = (sources[:, None] == jnp.arange(block_rows.shape[0])[None, :]).astype(jnp.bfloat16)
     picked = jnp.dot(selector, block_rows, preferred_element_type=jnp.float32)
     picked_four = picked.astype(jnp.bfloat16).reshape(prompts_here, length, ABLATED, HD)

time: 414 us -> 385 us (0.930)
  waiting for transfers between devices: 321 us -> 282 us
  local copies, waits for them, and re-layouts: 5.31 us -> 18.1 us
    all_gather x1, waiting for transfers between devices: 88.5 us -> 0.02 us  [body(): lax.all_gather(out_weight, 'batch', axis=0, tiled=True)]
    ppermute x0 -> x7, waiting for transfers between devices: none -> 78.7 us  [body(): lax.ppermute(ring[-1], 'batch', [(dev, (dev + 1) % 8) for dev in range(8)])]
    all_gather x1 -> x0, waiting for transfers between devices: 27.7 us -> none  [body(): block_rows = lax.all_gather(picked_cols, 'batch', axis=0, tiled=True)]
    concatenate x0 -> x1, local copies, waits for them, and re-layouts: none -> 10.6 us  [body(): jnp.roll(jnp.concatenate(ring[::-1], axis=0), (lax.axis_index('batch') +...]
  transfers between devices with their start and end apart: 5 -> 11, of which waited for: 5 -> 10; matrix products, arithmetic and copies ran while one was open for 1% -> 4% of each run, Pallas kernels for 0% -> 0%
where the time goes in v1:
time: 385 us; the launch traced here: 384 us
  waiting for transfers between devices  282 us (73%)
  matrix products  33.6 us (9%)
  blocking collectives  29 us (8%)
  local copies, waits for them, and re-layouts  18.1 us (5%)
  between operations  14.7 us (4%)
  other arithmetic  6.24 us (2%)
    psum x1, waiting for transfers between devices, body(): lax.psum(partial_value.astype(jnp.bfloat16), 'mp').astype(jnp.float32)  138 us
    ppermute x7, waiting for transfers between devices, body(): lax.ppermute(ring[-1], 'batch', [(dev, (dev + 1) % 8) for dev in range(8)])  78.7 us
    reduce_scatter x1, waiting for transfers between devices, body(): lax.psum_scatter(jnp.dot(block_rows, down_weight, preferred_element_type=...  40.4 us
    all_gather x1, waiting for transfers between devices, body(): block_rows = lax.all_gather(normed, 'batch', axis=0, tiled=True)  24.1 us
    all_gather x1, blocking collectives, body(): all_heads = lax.all_gather(head_block, 'mp', axis=2, tiled=True)  17.4 us
    psum x1, blocking collectives, body(): squares = lax.psum(jnp.sum(hidden_state * hidden_state, axis=1), 'mp')  11.7 us
    concatenate x1, local copies, waits for them, and re-layouts, body(): jnp.roll(jnp.concatenate(ring[::-1], axis=0), (lax.axis_index('batch') +...  10.6 us
    dot_general x1, matrix products, body(): jnp.dot(mixed_heads, lax.all_gather(out_weight, 'batch', axis=0, tiled=Tr...  8.91 us
  transfers between devices with their start and end apart: 11, of which 10 were waited for; matrix products, arithmetic and copies ran while one was open for 4% of the time, Pallas kernels for 0%

profile of v1, /device:TPU:0, one launch (start us, length us, event | category | flops | bytes accessed | tf_op | source)
XLA Modules:
  0.0 384.3 jit_solution(17536130863115360362)
XLA Ops:
  7.2 0.0 all-gather.3.cloned.1.call-start
  7.2 0.7 all-gather.3.cloned.1.call-update
  7.9 0.0 all-gather.5.cloned.1.call-start
  8.0 0.9 copy.29
  9.0 0.6 gather_fusion.2
  9.6 0.9 bitcast_bitcast_fusion.1
  10.4 0.6 gather_fusion.1
  11.0 0.3 fusion.7
  11.3 0.1 fusion.41
  11.4 0.3 fusion.9
  11.7 17.4 %all_gather.9 = bf16[1,64,4096]{2,1,0:T(8,128)(2,1)S(1)} all-gather(bf16[1,64,1024]{2,1,0:T(8,128)(2,1)S(1)} %bitcast.106), channel_id=1, replica_groups=mesh['batch'=8,'mp'=4] {'mp'}, dimensions={2}, use_global_device_ids=true | all-gather | bytes 655360 | tf_op jit(solution)/shard_map/all_gather | solution.py:53
  29.0 0.1 copy.30
  29.1 0.2 copy.23
  29.4 0.6 gather_fusion
  30.0 0.1 select_bitcast_fusion
  30.1 0.1 copy.24
  30.2 0.1 collective-permute-start
  30.3 12.3 %collective-permute-done = bf16[1,65536]{1,0:T(2,128)(2,1)S(1)} collective-permute-done((bf16[1,65536]{1,0:T(2,128)(2,1)S(1)}, bf16[1,65536]{1,0:T(2,128)(2,1)S(1)}, u32[]{:S(2)}, u32[]{:S(2)}) %collective-permute-start) | collective-permute-done | bytes 131104 | tf_op jit(solution)/shard_map/ppermute | solution.py:62
  42.6 10.8 %collective-permute-done.1 = bf16[1,65536]{1,0:T(2,128)(2,1)S(1)} collective-permute-done((bf16[1,65536]{1,0:T(2,128)(2,1)S(1)}, bf16[1,65536]{1,0:T(2,128)(2,1)S(1)}, u32[]{:S(2)}, u32[]{:S(2)}) %collective-permute-start.1) | collective-permute-done | bytes 131104 | tf_op jit(solution)/shard_map/ppermute | solution.py:62
  53.4 0.7 copy-done.3
  54.1 7.8 %collective-permute-done.2 = bf16[1,65536]{1,0:T(2,128)(2,1)S(1)} collective-permute-done((bf16[1,65536]{1,0:T(2,128)(2,1)S(1)}, bf16[1,65536]{1,0:T(2,128)(2,1)S(1)}, u32[]{:S(2)}, u32[]{:S(2)}) %collective-permute-start.2) | collective-permute-done | bytes 131104 | tf_op jit(solution)/shard_map/ppermute | solution.py:62
  61.9 0.7 copy-done.4
  62.6 12.3 %collective-permute-done.3 = bf16[1,65536]{1,0:T(2,128)(2,1)S(1)} collective-permute-done((bf16[1,65536]{1,0:T(2,128)(2,1)S(1)}, bf16[1,65536]{1,0:T(2,128)(2,1)S(1)}, u32[]{:S(2)}, u32[]{:S(2)}) %collective-permute-start.3) | collective-permute-done | bytes 131104 | tf_op jit(solution)/shard_map/ppermute | solution.py:62
  74.8 0.7 copy-done.5
  75.6 12.3 %collective-permute-done.4 = bf16[1,65536]{1,0:T(2,128)(2,1)S(1)} collective-permute-done((bf16[1,65536]{1,0:T(2,128)(2,1)S(1)}, bf16[1,65536]{1,0:T(2,128)(2,1)S(1)}, u32[]{:S(2)}, u32[]{:S(2)}) %collective-permute-start.4) | collective-permute-done | bytes 131104 | tf_op jit(solution)/shard_map/ppermute | solution.py:62
  87.8 0.7 copy-done.6
  88.5 12.3 %collective-permute-done.5 = bf16[1,65536]{1,0:T(2,128)(2,1)S(1)} collective-permute-done((bf16[1,65536]{1,0:T(2,128)(2,1)S(1)}, bf16[1,65536]{1,0:T(2,128)(2,1)S(1)}, u32[]{:S(2)}, u32[]{:S(2)}) %collective-permute-start.5) | collective-permute-done | bytes 131104 | tf_op jit(solution)/shard_map/ppermute | solution.py:62
  100.8 0.7 dynamic-slice.2
  102.1 0.1 fusion.29
  102.2 11.0 %collective-permute-done.6 = bf16[1,65536]{1,0:T(2,128)(2,1)} collective-permute-done((bf16[1,65536]{1,0:T(2,128)(2,1)S(1)}, bf16[1,65536]{1,0:T(2,128)(2,1)}, u32[]{:S(2)}, u32[]{:S(2)}) %collective-permute-start.6) | collective-permute-done | bytes 131104 | tf_op jit(solution)/shard_map/ppermute | solution.py:62
  113.2 10.6 %concatenate.10 = bf16[16,65536]{1,0:T(8,128)(2,1)S(1)} concatenate(bf16[1,65536]{1,0:T(2,128)(2,1)} %collective-permute-done.6, bf16[1,65536]{1,0:T(2,128)(2,1)} %copy-done.7, bf16[1,65536]{1,0:T(2,128)(2,1)} %copy-done.6, bf16[1,65536]{1,0:T(2,128)(2,1)} %copy-done.5, bf16[1,65536]{1,0:T(2,128)(2,1)} %copy-done.4, bf16[1,65536]{1,0:T(2,128)(2,1)} %copy-done.3, ...), dimensions={0} | concatenate | bytes 4194304 | tf_op jit(solution)/shard_map/jit(_roll_dynamic)/concatenate | solution.py:63
  123.8 0.4 fusion.11
  124.3 0.4 fusion.10
  124.7 0.0 all-gather.3.cloned.1.call-done
  124.7 8.9 %multiply_reduce_fusion = (f32[64]{0:T(128)S(1)}, f32[64,2048]{1,0:T(8,128)S(1)}) fusion(bf16[1,64,2048]{2,1,0:T(8,128)(2,1)S(1)} %copy-done.2, bf16[4096,2048]{1,0:T(8,128)(2,1)} %all-gather.3.cloned.1.call-done, bf16[8,8,32,128]{3,2,1,0:T(8,128)(2,1)S(1)} %bitcast.103), kind=kOutput, calls=%fused_computation.28 | convolution fusion | flops 1074266112 | bytes 18088192 | tf_op jit(solution)/shard_map/dot_general | solution.py:79
  133.6 11.7 %psum.14 = f32[64]{0:T(128)S(1)} all-reduce(f32[64]{0:T(128)S(1)} %get-tuple-element.16), channel_id=1, replica_groups=mesh['batch'=8,'mp'=4] {'mp'}, use_global_device_ids=true, to_apply=%region_4.6 | all-reduce | flops 64 | bytes 512 | tf_op jit(solution)/shard_map/psum | solution.py:86
  145.3 0.8 multiply_convert_fusion
  146.2 0.0 all-gather.5.cloned.1.call-update
  146.2 0.2 all-reduce.2.cloned.1.call-start
  146.4 24.1 %all-gather.5.cloned.1.call-done = bf16[512,2048]{1,0:T(8,128)(2,1)} async-done(((bf16[64,2048]{1,0:T(8,128)(2,1)}), bf16[512,2048]{1,0:T(8,128)(2,1)}) %all-gather.5.cloned.1.call-update) | async-done | bytes 2097168 | tf_op jit(solution)/shard_map/all_gather | solution.py:89
  170.6 7.8 %convolution_convert_fusion.1 = bf16[512,1792]{1,0:T(8,128)(2,1)S(1)} fusion(bf16[512,2048]{1,0:T(8,128)(2,1)} %all-gather.5.cloned.1.call-done, bf16[2048,1792]{1,0:T(8,128)(2,1)} %param.22), kind=kOutput, calls=%fused_computation.8 | convolution fusion | flops 3759013888 | bytes 11272192 | tf_op jit(solution)/shard_map/dot_general | solution.py:91
  178.4 7.0 %convolution_convert_fusion.2 = bf16[512,1792]{1,0:T(8,128)(2,1)S(1)} fusion(bf16[512,2048]{1,0:T(8,128)(2,1)S(1)} %copy-done.10, bf16[2048,1792]{1,0:T(8,128)(2,1)} %param.21), kind=kOutput, calls=%fused_computation.9 | convolution fusion | flops 3759013888 | bytes 11272192 | tf_op jit(solution)/shard_map/dot_general | solution.py:90
  185.4 2.1 pad_maximum_fusion
  187.6 0.0 reduce-scatter.2.cloned.1.call-start
  187.6 138.2 %all-reduce.2.cloned.1.call-done = bf16[512,3584]{1,0:T(8,128)(2,1)} async-done(((bf16[512,3584]{1,0:T(8,128)(2,1)}), bf16[512,3584]{1,0:T(8,128)(2,1)}) %all-reduce.2.cloned.1.call-update) | async-done | bytes 3670032 | tf_op jit(solution)/shard_map/psum | solution.py:94
  325.8 3.0 convert_element_type.62
  328.8 8.5 %convolution_convert_fusion = bf16[512,2048]{1,0:T(8,128)(2,1)} fusion(bf16[1792,2048]{1,0:T(8,128)(2,1)} %param.23, f32[512,3584]{1,0:T(8,128)S(1)} %convert_element_type.62), kind=kOutput, calls=%fused_computation.7 | convolution fusion | flops 3764649984 | bytes 16777216 | tf_op jit(solution)/shard_map/dot_general | solution.py:98
  337.3 40.4 %reduce-scatter.2.cloned.1.call-done = bf16[64,2048]{1,0:T(8,128)(2,1)} async-done(((bf16[512,2048]{1,0:T(8,128)(2,1)}), bf16[64,2048]{1,0:T(8,128)(2,1)}) %reduce-scatter.2.cloned.1.call-update) | async-done | bytes 262160 | tf_op jit(solution)/shard_map/reduce_scatter | solution.py:97
  (39 shorter events, 0.3 us)
Async XLA Ops:
  7.2 1.8 copy-start
  7.2 117.5 %all-gather.3.cloned.1.call-start = ((), (), s32[]{:S(2)}) async-start(), calls=%async_computation.1 | async-start | bytes 18874368 | tf_op jit(solution)/shard_map/all_gather | solution.py:81
  7.9 21.4 %copy-start.9 = (s32[8]{0:T(128)S(1)}, s32[8]{0:T(128)}, u32[]{:S(2)}) copy-start(s32[8]{0:T(128)} %param.18) | copy-start | bytes 100
  7.9 162.7 %all-gather.5.cloned.1.call-start = ((), (), s32[]{:S(2)}) async-start(), calls=%async_computation.2 | async-start | bytes 2359296 | tf_op jit(solution)/shard_map/all_gather | solution.py:89
  8.9 91.9 %copy-start.11 = (s32[8]{0:T(128)S(1)}, s32[8]{0:T(128)}, u32[]{:S(2)}) copy-start(s32[8]{0:T(128)} %param.17) | copy-start | bytes 100
  30.2 12.3 %collective-permute-start = (bf16[1,65536]{1,0:T(2,128)(2,1)S(1)}, bf16[1,65536]{1,0:T(2,128)(2,1)S(1)}, u32[]{:S(2)}, u32[]{:S(2)}) collective-permute-start(bf16[1,65536]{1,0:T(2,128)(2,1)S(1)} %reshape.199), channel_id=1, source_target_pairs={{0,4},{4,8},{8,12},{12,16},{16,20},{20,24},{24,28},{28,0},{1,5},{5... | collective-permute-start | bytes 393224 | tf_op jit(solution)/shard_map/ppermute | solution.py:62
  42.6 10.8 %collective-permute-start.1 = (bf16[1,65536]{1,0:T(2,128)(2,1)S(1)}, bf16[1,65536]{1,0:T(2,128)(2,1)S(1)}, u32[]{:S(2)}, u32[]{:S(2)}) collective-permute-start(bf16[1,65536]{1,0:T(2,128)(2,1)S(1)} %collective-permute-done), channel_id=1, source_target_pairs={{0,4},{4,8},{8,12},{12,16},{16,20},{20,24},{24,28},{28,0},{1,5},{5... | collective-permute-start | bytes 393224 | tf_op jit(solution)/shard_map/ppermute | solution.py:62
  53.4 0.7 copy-start.3
  54.1 7.8 %collective-permute-start.2 = (bf16[1,65536]{1,0:T(2,128)(2,1)S(1)}, bf16[1,65536]{1,0:T(2,128)(2,1)S(1)}, u32[]{:S(2)}, u32[]{:S(2)}) collective-permute-start(bf16[1,65536]{1,0:T(2,128)(2,1)S(1)} %collective-permute-done.1), channel_id=1, source_target_pairs={{0,4},{4,8},{8,12},{12,16},{16,20},{20,24},{24,28},{28,0},{1,5},{5... | collective-permute-start | bytes 393224 | tf_op jit(solution)/shard_map/ppermute | solution.py:62
  61.9 0.7 copy-start.4
  62.6 12.3 %collective-permute-start.3 = (bf16[1,65536]{1,0:T(2,128)(2,1)S(1)}, bf16[1,65536]{1,0:T(2,128)(2,1)S(1)}, u32[]{:S(2)}, u32[]{:S(2)}) collective-permute-start(bf16[1,65536]{1,0:T(2,128)(2,1)S(1)} %collective-permute-done.2), channel_id=1, source_target_pairs={{0,4},{4,8},{8,12},{12,16},{16,20},{20,24},{24,28},{28,0},{1,5},{5... | collective-permute-start | bytes 393224 | tf_op jit(solution)/shard_map/ppermute | solution.py:62
  74.8 0.7 copy-start.5
  75.6 12.3 %collective-permute-start.4 = (bf16[1,65536]{1,0:T(2,128)(2,1)S(1)}, bf16[1,65536]{1,0:T(2,128)(2,1)S(1)}, u32[]{:S(2)}, u32[]{:S(2)}) collective-permute-start(bf16[1,65536]{1,0:T(2,128)(2,1)S(1)} %collective-permute-done.3), channel_id=1, source_target_pairs={{0,4},{4,8},{8,12},{12,16},{16,20},{20,24},{24,28},{28,0},{1,5},{5... | collective-permute-start | bytes 393224 | tf_op jit(solution)/shard_map/ppermute | solution.py:62
  87.8 0.7 copy-start.6
  88.5 12.3 %collective-permute-start.5 = (bf16[1,65536]{1,0:T(2,128)(2,1)S(1)}, bf16[1,65536]{1,0:T(2,128)(2,1)S(1)}, u32[]{:S(2)}, u32[]{:S(2)}) collective-permute-start(bf16[1,65536]{1,0:T(2,128)(2,1)S(1)} %collective-permute-done.4), channel_id=1, source_target_pairs={{0,4},{4,8},{8,12},{12,16},{16,20},{20,24},{24,28},{28,0},{1,5},{5... | collective-permute-start | bytes 393224 | tf_op jit(solution)/shard_map/ppermute | solution.py:62
  100.8 1.4 copy-start.7
  100.8 12.4 %collective-permute-start.6 = (bf16[1,65536]{1,0:T(2,128)(2,1)S(1)}, bf16[1,65536]{1,0:T(2,128)(2,1)}, u32[]{:S(2)}, u32[]{:S(2)}) collective-permute-start(bf16[1,65536]{1,0:T(2,128)(2,1)S(1)} %collective-permute-done.5), channel_id=1, source_target_pairs={{0,4},{4,8},{8,12},{12,16},{16,20},{20,24},{24,28},{28,0},{1,5},{5... | collective-permute-start | bytes 393224 | tf_op jit(solution)/shard_map/ppermute | solution.py:62
  102.2 22.5 %copy-start.2 = (bf16[1,64,2048]{2,1,0:T(8,128)(2,1)S(1)}, bf16[1,64,2048]{2,1,0:T(8,128)(2,1)}, u32[]{:S(2)}) copy-start(bf16[1,64,2048]{2,1,0:T(8,128)(2,1)} %param.13) | copy-start | bytes 786436
  124.7 20.6 %copy-start.8 = (f32[2048]{0:T(1024)S(1)}, f32[2048]{0:T(1024)}, u32[]{:S(2)}) copy-start(f32[2048]{0:T(1024)} %param.20) | copy-start | bytes 24580
  146.2 179.6 %all-reduce.2.cloned.1.call-start = ((), (), s32[]{:S(2)}) async-start(), calls=%async_computation.3 | async-start | bytes 7340032 | tf_op jit(solution)/shard_map/psum | solution.py:94
  170.6 7.8 %copy-start.10 = (bf16[512,2048]{1,0:T(8,128)(2,1)S(1)}, bf16[512,2048]{1,0:T(8,128)(2,1)}, u32[]{:S(2)}) copy-start(bf16[512,2048]{1,0:T(8,128)(2,1)} %all-gather.5.cloned.1.call-done) | copy-start | bytes 6291460
  187.6 190.2 %reduce-scatter.2.cloned.1.call-start = ((), (), s32[]{:S(2)}) async-start(), calls=%async_computation.4 | async-start | bytes 2359296 | tf_op jit(solution)/shard_map/reduce_scatter | solution.py:97
  328.8 49.0 %copy-start.1 = (bf16[1,64,512]{2,1,0:T(8,128)(2,1)S(1)}, bf16[1,64,512]{2,1,0:T(8,128)(2,1)}, u32[]{:S(2)}) copy-start(bf16[1,64,512]{2,1,0:T(8,128)(2,1)} %param.15) | copy-start | bytes 196612
Sparse Core Ops, SparseCore 0:
  9.9 109.5 all-gather.2
  146.3 24.2 all-gather.4
  187.7 138.0 all-reduce.1
  337.5 40.2 reduce-scatter.1
